TPU v7x, 512 devices: a whole 4x4x16 slice. The times are simulated.
512 devices in a mesh: row: 16 (over x, y_hi, core), col: 16 (over z), atom: 2 (over y_lo).
Axes of the slice: x: 4, y: 4 (y_hi: 2, y_lo: 2; y = y_hi * 2 + y_lo), z: 16, core: 2. Of those that a mesh axis runs over, the one named last changes fastest.
Arguments:
- proj: bfloat16 [24, 104, 12288], P('atom', None, 'row'), may hold values from -1.5 to 1.5
- nbr: int32 [24, 96], P('atom', 'row'), may hold values from -1 to 117, as said below
- dh: float32 [118, 8, 13, 13], P('atom'), may hold values from -1 to 1, as said below
Outputs:
- correction: float32 [12288, 12288], P('row', ('col', 'atom'))
Inputs may be any that keep to these rules, and one draw needn't show every extreme that they name: `nbr`: rows s * 12 to (s + 1) * 12 - 1 hold, for each basis tile, its neighbours among atom tiles s * 59 to (s + 1) * 59 - 1: live entries first, distinct and rising, then -1 in empty slots; every list has at least 6 live entries, and in every subset some list has all 12 live. dh[A, a] is symmetric.
All inputs are finite; a program needn't handle non-finite values.
Results may differ from a plain program's by a relative error of at most 0.0029.
Values may be sent and summed in bfloat16 or wider, within the bound.
A program may use at most 64 MiB of HBM per device.

v0:
```python
import jax
import jax.numpy as jnp
from jax import lax
from jax.sharding import PartitionSpec as P


def from_root(value, axis, source):
    kept = jnp.where(lax.axis_index(axis) == source, value, 0).astype(value.dtype)
    return lax.psum(kept, axis)


def form_products(blockp, blockid, table, base):
    lcount, ap, rows = blockp.shape
    tiles = blockid.shape[1]
    width = rows // tiles
    natoms, atb, npj, unused = table.shape
    safe = jnp.clip(blockid - base, 0, natoms - 1).astype(jnp.int32)
    chosen = table[safe]
    ptile = blockp.reshape(lcount, atb, npj, tiles, width).astype(jnp.float32)
    prod = jnp.einsum("ltaij,lajtb->laitb", chosen, ptile, precision=lax.Precision.HIGHEST)
    return prod.reshape(lcount, ap, rows).astype(jnp.bfloat16)


def assemble(rowp, rowid, colq, colid):
    lcount, ap, rows = rowp.shape
    rtiles = rowid.shape[1]
    width = rows // rtiles
    ctiles = colid.shape[1]
    mcount = colq.shape[0]
    ptile = rowp.reshape(lcount, ap, rtiles, width)
    qtile = jnp.moveaxis(colq.reshape(mcount, ap, ctiles, width), 2, 0)
    idtile = jnp.moveaxis(colid, 1, 0)

    def one_tile(args):
        qpiece, idpiece = args
        match = (jnp.transpose(rowid)[:, :, None] == idpiece[None, None, :]) & (
            idpiece[None, None, :] >= 0
        )
        match = match.astype(jnp.bfloat16).reshape(rtiles * lcount, mcount)
        picked = jnp.dot(
            match, qpiece.reshape(mcount, ap * width), preferred_element_type=jnp.float32
        )
        picked = picked.astype(jnp.bfloat16).reshape(rtiles, lcount, ap, width)
        return jnp.einsum("lptx,tlpb->txb", ptile, picked, preferred_element_type=jnp.float32)

    blocks = lax.map(one_tile, (qtile, idtile))
    return jnp.transpose(blocks, (1, 2, 0, 3)).reshape(rows, ctiles * width)


def on_device(proj, nbr, dh):
    subset = lax.axis_index("atom")
    base = subset * dh.shape[0]
    column = lax.axis_index("col")
    colp, colid = (from_root(proj, "row", column), from_root(nbr, "row", column))
    colq = form_products(colp, colid, dh, base)
    partial_block = assemble(proj, nbr, colq, colid)
    return lax.psum_scatter(partial_block, "atom", scatter_dimension=1, tiled=True)


def solution(mesh):
    placed = (P("atom", None, "row"), P("atom", "row"), P("atom", None, None, None))
    return jax.shard_map(
        on_device, mesh=mesh, in_specs=placed, out_specs=P("row", ("col", "atom")), check_vma=False
    )
```

profile of v0, /device:TPU:1, one launch (start us, length us, event | category | flops | bytes accessed | tf_op | source)
XLA Modules:
  0.0 272.7 jit_solution(13805355276471280590)
XLA Ops:
  6.5 1.4 broadcast_select_fusion
  7.9 4.2 %reshape.33 = bf16[12,8,13,6,128]{4,3,2,1,0:T(8,128)(2,1)S(1)} reshape(bf16[12,104,768]{2,1,0:T(8,128)(2,1)} %broadcast_select_fusion) | data formatting | bytes 3833856 | tf_op jit(solution)/shard_map/reshape | solution.py:19
  12.1 2.0 copy.7
  14.8 12.4 %psum.14 = s32[12,6]{0,1:T(8,128)S(1)} all-reduce(s32[12,6]{0,1:T(8,128)S(1)} %broadcast_select_fusion.1), channel_id=1, replica_groups=mesh['row'=16,'col'=16,'atom'=2] {'row'}, use_global_device_ids=true, to_apply=%region_1.2 | all-reduce | flops 72 | bytes 576 | tf_op jit(solution)/shard_map/psum | solution.py:9
  27.4 2.6 copy.9
  30.1 2.7 gather_fusion
  32.7 1.9 copy_bitcast_fusion.1
  34.6 145.9 %all-reduce.2.cloned.1.call-done = bf16[12,8,13,6,128]{4,2,3,1,0:T(8,128)(2,1)} async-done(((bf16[12,8,13,6,128]{4,2,3,1,0:T(8,128)(2,1)}), bf16[12,8,13,6,128]{4,2,3,1,0:T(8,128)(2,1)}) %all-reduce.2.cloned.1.call-update) | async-done | bytes 1916944 | tf_op jit(solution)/shard_map/psum | solution.py:9
  180.5 5.8 %convert_bitcast_fusion = bf16[12,8,13,6,128]{4,2,3,1,0:T(8,128)(2,1)S(1)} fusion(bf16[12,8,13,6,128]{4,2,3,1,0:T(8,128)(2,1)} %all-reduce.2.cloned.1.call-done, f32[12,6,8,13,13]{4,2,3,1,0:T(8,128)} %bitcast.68), kind=kOutput, calls=%fused_computation.17 | convolution fusion | flops 150478848 | bytes 4223232 | tf_op jit(solution)/shard_map/ltaij,lajtb->laitb/dot_general | solution.py:20
  186.3 2.1 copy.11
  188.3 4.1 %convert_element_type.19 = bf16[12,104,6,128]{3,1,2,0:T(8,128)(2,1)} reshape(bf16[12,8,13,6,128]{4,2,1,3,0:T(8,128)(2,1)} %copy.11) | data formatting | bytes 3833856 | tf_op jit(solution)/shard_map/convert_element_type | solution.py:21
  192.4 22.5 %while.10 = (s32[]{:T(128)}, f32[6,6,128,128]{2,3,1,0:T(8,128)}, s32[12,6]{0,1:T(8,128)S(1)}, s32[6,12]{1,0:T(8,128)S(1)}, bf16[6,12,104,128]{3,2,0,1:T(8,128)(2...) while((s32[]{:T(128)}, f32[6,6,128,128]{2,3,1,0:T(8,128)}, s32[12,6]{0,1:T(8,128)S(1)}, ...), condition=%wide.region_3.4_spmd, body=%wide.region_2.3_spmd.sunk | while | flops 269330112 | bytes 12535399 | solution.py:46
  192.4 1.0 dynamic-slice_bitcast_fusion.2
  194.6 1.6 fusion.29
  196.2 1.0 dynamic-slice_bitcast_fusion.2
  198.4 1.5 fusion.29
  199.9 1.0 dynamic-slice_bitcast_fusion.2
  202.1 1.6 fusion.29
  205.8 1.6 fusion.29
  209.6 1.6 fusion.29
  213.4 1.6 fusion.29
  214.9 2.4 copy.14
  217.3 2.0 copy.27
  219.3 46.6 %reduce-scatter.2.cloned.1.call-done = f32[768,384]{1,0:T(8,128)} async-done(((f32[768,768]{1,0:T(8,128)}), f32[768,384]{1,0:T(8,128)}) %reduce-scatter.2.cloned.1.call-update) | async-done | bytes 1179664 | tf_op jit(solution)/shard_map/reduce_scatter | solution.py:57
  (51 shorter events, 10.8 us)
Async XLA Ops:
  6.5 174.0 %all-reduce.2.cloned.1.call-start = ((), (), s32[]{:S(2)}) async-start(), calls=%async_computation.1 | async-start | bytes 4718592 | tf_op jit(solution)/shard_map/psum | solution.py:9
  14.1 0.7 copy-start
  14.1 251.7 %reduce-scatter.2.cloned.1.call-start = ((), (), s32[]{:S(2)}) async-start(), calls=%async_computation.2 | async-start | bytes 3538944 | tf_op jit(solution)/shard_map/reduce_scatter | solution.py:57
Sparse Core Ops, SparseCore 0:
  14.3 166.1 all-reduce.1
  219.4 46.4 reduce-scatter.1
where the time goes:
time: 273 us
  waiting for transfers between devices  193 us (71%)
  local copies, waits for them, and re-layouts  33.3 us (12%)
  matrix products  19.3 us (7%)
  between operations  13.5 us (5%)
  blocking collectives  12.4 us (5%)
    psum x1, waiting for transfers between devices, from_root(): return lax.psum(kept, axis)  146 us
    reduce_scatter x1, waiting for transfers between devices, on_device(): lax.psum_scatter(partial_block, 'atom', scatter_dimension=1, tiled=True)  46.6 us
    psum x1, blocking collectives, from_root(): return lax.psum(kept, axis)  12.4 us
    dot_general x6, matrix products, one_tile(): jnp.einsum('lptx,tlpb->txb', ptile, picked, preferred_element_type=jnp.fl...  9.36 us
    while x24, local copies, waits for them, and re-layouts  8.21 us
    reshape x2, local copies, waits for them, and re-layouts, form_products(): ptile = blockp.reshape(lcount, atb, npj, tiles, width).astype(jnp.float32)  6.17 us
    convert_element_type x2, local copies, waits for them, and re-layouts, form_products(): return prod.reshape(lcount, ap, rows).astype(jnp.bfloat16)  6.16 us
    dot_general x1, matrix products, form_products(): jnp.einsum('ltaij,lajtb->laitb', chosen, ptile, precision=lax.Precision.H...  5.76 us
  transfers between devices with their start and end apart: 2, of which 2 were waited for; matrix products, arithmetic and copies ran while one was open for 3% of the time, Pallas kernels for 0%

commit v1 on v0

v1 whole, which is shorter than its diff:
```python
import functools

import jax
import jax.numpy as jnp
from jax import lax
from jax.experimental import pallas as pl
from jax.experimental.pallas import tpu as pltpu
from jax.sharding import PartitionSpec as P

MESH = pl.DeviceIdType.MESH
BT = 128
PAD = 16


def kernel(proj, dh, ids, out, pbuf, colb, dhv, xpad, dhi, dlo, pt, sel, q, acc, xsend, xrecv,
           colx, idv, ids_s, lsem, dsem, isem, nsend, nrecv, rsem, ssem, xssem, xrsem):
    slots, ap, _ = proj.shape
    nats, atb, npj, _ = dh.shape
    tiles = pbuf.shape[0]
    half = tiles // 2
    part = slots // 4
    row, c, a = lax.axis_index("row"), lax.axis_index("col"), lax.axis_index("atom")
    x, h, k = row // 4, (row // 2) % 2, row % 2
    xs, hs, ks = c // 4, (c // 2) % 2, c % 2
    is_root = row == c
    root_chip = (row // 2) == (c // 2)

    def dev(x_, h_, k_):
        return (x_ * 4 + h_ * 2 + k_, c, a)

    def tile_of(t):
        return (t + half * (1 - a)) % tiles

    bar = pltpu.get_barrier_semaphore()
    for i in range(1, 16):
        pl.semaphore_signal(bar, inc=1, device_id=((row + i) % 16, c, a), device_id_type=MESH)
    pl.semaphore_signal(bar, inc=1, device_id=(row, c, 1 - a), device_id_type=MESH)

    loads = [
        pltpu.make_async_copy(proj.at[:, :, pl.ds(i * BT, BT)], pbuf.at[i], lsem.at[i])
        for i in range(tiles)
    ]
    for cp in loads:
        cp.start()
    dcopy = pltpu.make_async_copy(dh, dhv, dsem)
    dcopy.start()
    for cp in loads:
        cp.wait()
    pl.semaphore_wait(bar, 16)

    def quarter(buf, t, qx):
        return buf.at[t, pl.ds(part * qx, part)]

    def send(src, t, qx, slot, target):
        return pltpu.make_async_remote_copy(
            src_ref=src, dst_ref=quarter(colb, t, qx), send_sem=ssem.at[t, slot],
            recv_sem=rsem.at[t, qx], device_id=target, device_id_type=MESH)

    def root_ids(i):
        return pltpu.make_async_remote_copy(
            src_ref=ids.at[pl.ds(16, 16)], dst_ref=colx, send_sem=nsend.at[i - 1],
            recv_sem=nrecv, device_id=((row + i) % 16, c, a), device_id_type=MESH)

    def root_sends(t):
        kt = t % 2
        tile = tile_of(t)
        own = quarter(pbuf, tile, xs)
        copies = []
        for n, d in enumerate((1, 3, 2)):
            qx = (xs + d) % 4
            copies.append(send(quarter(pbuf, tile, qx), t, qx, n, dev(qx, hs, kt)))
        copies.append(send(own, t, xs, 3, dev(xs, 1 - hs, kt)))
        for n, d in enumerate((1, 3, 2)):
            copies.append(send(own, t, xs, 4 + n, dev((xs + d) % 4, hs, kt)))
        for qx in range(4):
            copies.append(send(quarter(pbuf, tile, qx), t, qx, 7 + qx, dev(xs, hs, 1 - ks)))
        return copies

    @pl.when(is_root)
    def _():
        for i in range(1, 16):
            root_ids(i).start()
        pltpu.make_async_copy(ids.at[pl.ds(16, 16)], colx, nrecv).start()

        def step(t, carry):
            for cp in root_sends(t):
                cp.start()
            for qx in range(4):
                pltpu.make_async_copy(
                    quarter(pbuf, tile_of(t), qx), quarter(colb, t, qx), rsem.at[t, qx]).start()
            return carry

        lax.fori_loop(0, tiles, step, 0)

    def arrived(t, qx):
        pltpu.make_async_copy(quarter(colb, t, qx), quarter(colb, t, qx), rsem.at[t, qx]).wait()

    def relay(t):
        return (k == t % 2) & jnp.logical_not(root_chip)

    def relay_first(t):
        mine = quarter(colb, t, x)
        cross = send(mine, t, x, 0, dev(x, 1 - hs, k))
        along = [(send(mine, t, x, 1 + n, dev((x + d) % 4, h, k)),
                  jnp.logical_not((h == hs) & ((x + d) % 4 == xs)))
                 for n, d in enumerate((1, 3, 2))]
        twin = send(mine, t, x, 4, dev(x, h, 1 - k))
        return cross, along, twin

    def relay_rest(t):
        return [((x + d) % 4, send(quarter(colb, t, (x + d) % 4), t, (x + d) % 4, 5 + n,
                                   dev(x, h, 1 - k)))
                for n, d in enumerate((1, 3, 2))]

    def forward_first(t):
        @pl.when(relay(t))
        def _():
            arrived(t, x)
            cross, along, twin = relay_first(t)

            @pl.when(h == hs)
            def _():
                cross.start()

            for cp, needed in along:
                @pl.when(needed)
                def _():
                    cp.start()

            twin.start()

    def forward_rest(t):
        @pl.when(relay(t))
        def _():
            for qx, cp in relay_rest(t):
                arrived(t, qx)
                cp.start()

        @pl.when(jnp.logical_not(relay(t)))
        def _():
            for qx in range(4):
                arrived(t, qx)

    dcopy.wait()
    xpad[...] = jnp.zeros_like(xpad)

    def table(i, carry):
        xpad[:, 0:npj, 0:npj] = dhv[i]
        for b in range(atb):
            v = xpad[b]
            if b:
                v = pltpu.roll(v, npj * b, 1)
            hi = v.astype(jnp.bfloat16)
            dhi[i, b * PAD:(b + 1) * PAD, :] = hi
            dlo[i, b * PAD:(b + 1) * PAD, :] = (v - hi.astype(jnp.float32)).astype(jnp.bfloat16)
        return carry

    lax.fori_loop(0, nats, table, 0)

    forward_first(0)
    forward_first(1)

    pidx = lax.broadcasted_iota(jnp.int32, (ap, BT), 0)
    sidx = lax.broadcasted_iota(jnp.int32, (ap, BT), 1)
    spread = ((sidx >> 4) * npj + (sidx & 15) == pidx) & ((sidx & 15) < npj)
    spread = spread.astype(jnp.float32).astype(jnp.bfloat16)

    def flip(u, carry):
        for l in range(slots):
            pt[u, l] = lax.dot_general(
                pbuf[u, l], spread, (((0,), (0,)), ((), ())),
                preferred_element_type=jnp.float32).astype(jnp.bfloat16)
        pt[u, slots] = jnp.zeros((BT, BT), jnp.bfloat16)
        return carry

    lax.fori_loop(0, tiles, flip, 0)

    pltpu.make_async_copy(ids.at[pl.ds(16, 16)], colx, nrecv).wait()
    cols = colx[...]
    found = jnp.full((16, BT), slots, jnp.int32)
    for l in range(slots):
        same = (ids[l:l + 1, :] == cols) & (cols >= 0)
        found = jnp.where(same, l, found)
    idv[0:16, :] = found
    idv[16:32, :] = jnp.clip(cols - a * nats, 0, nats - 1)
    icopy = pltpu.make_async_copy(idv, ids_s, isem)
    icopy.start()
    icopy.wait()

    def exchange(t):
        return pltpu.make_async_remote_copy(
            src_ref=xsend.at[t], dst_ref=xrecv.at[t], send_sem=xssem.at[t], recv_sem=xrsem.at[t],
            device_id=(row, c, 1 - a), device_id_type=MESH)

    def step(t, carry):
        @pl.when(t + 2 < tiles)
        def _():
            forward_first(t + 2)

        forward_rest(t)
        tile = tile_of(t)
        for m in range(slots):
            i = ids_s[16 + m, tile * tiles]
            piece = colb[t, m]
            prod = jnp.dot(dhi[i][:, :ap], piece, preferred_element_type=jnp.float32)
            prod += jnp.dot(dlo[i][:, :ap], piece, preferred_element_type=jnp.float32)
            q[m * BT:(m + 1) * BT, :] = prod.astype(jnp.bfloat16)
        for u in range(tiles):
            for m in range(slots):
                l = ids_s[m, tile * tiles + u]
                sel[u * BT:(u + 1) * BT, m * BT:(m + 1) * BT] = pt[u, l]
        block = jnp.dot(sel[...], q[...], preferred_element_type=jnp.float32)

        @pl.when(t < half)
        def _():
            xsend[t] = block.astype(jnp.bfloat16)
            exchange(t).start()

        @pl.when(t >= half)
        def _():
            acc[t - half] = block

        return carry

    lax.fori_loop(0, tiles, step, 0)

    for j in range(half):
        exchange(j).wait_recv()
        out[:, j * BT:(j + 1) * BT] = acc[j] + xrecv[j].astype(jnp.float32)

    for j in range(half):
        exchange(j).wait_send()

    @pl.when(is_root)
    def _():
        for i in range(1, 16):
            root_ids(i).wait_send()

        def drain(t, carry):
            for cp in root_sends(t):
                cp.wait_send()
            return carry

        lax.fori_loop(0, tiles, drain, 0)

    def drain(t, carry):
        @pl.when(relay(t))
        def _():
            cross, along, twin = relay_first(t)

            @pl.when(h == hs)
            def _():
                cross.wait_send()

            for cp, needed in along:
                @pl.when(needed)
                def _():
                    cp.wait_send()

            twin.wait_send()
            for _, cp in relay_rest(t):
                cp.wait_send()

        return carry

    lax.fori_loop(0, tiles, drain, 0)


def on_device(proj, nbr, dh):
    slots, ap, rows = proj.shape
    tiles = nbr.shape[1]
    nats, atb, npj, _ = dh.shape
    half = tiles // 2
    rowx = jnp.tile(nbr, (1, tiles))
    colx = jnp.repeat(nbr, tiles, axis=1)
    pad = ((0, 16 - slots), (0, BT - tiles * tiles))
    ids = jnp.concatenate([jnp.pad(v, pad, constant_values=-1) for v in (rowx, colx)], axis=0)
    bf, f32 = jnp.bfloat16, jnp.float32
    return pl.pallas_call(
        kernel,
        out_shape=jax.ShapeDtypeStruct((rows, half * BT), f32),
        in_specs=[pl.BlockSpec(memory_space=pl.ANY), pl.BlockSpec(memory_space=pl.ANY),
                  pl.BlockSpec(memory_space=pltpu.VMEM)],
        out_specs=pl.BlockSpec(memory_space=pltpu.VMEM),
        scratch_shapes=[
            pltpu.VMEM((tiles, slots, ap, BT), bf),
            pltpu.VMEM((tiles, slots, ap, BT), bf),
            pltpu.VMEM(dh.shape, f32),
            pltpu.VMEM((atb, PAD, BT), f32),
            pltpu.VMEM((nats, atb * PAD, BT), bf),
            pltpu.VMEM((nats, atb * PAD, BT), bf),
            pltpu.VMEM((tiles, slots + 1, BT, BT), bf),
            pltpu.VMEM((rows, slots * BT), bf),
            pltpu.VMEM((slots * BT, BT), bf),
            pltpu.VMEM((half, rows, BT), f32),
            pltpu.VMEM((half, rows, BT), bf),
            pltpu.VMEM((half, rows, BT), bf),
            pltpu.VMEM((16, BT), jnp.int32),
            pltpu.VMEM((32, BT), jnp.int32),
            pltpu.SMEM((32, BT), jnp.int32),
            pltpu.SemaphoreType.DMA((tiles,)),
            pltpu.SemaphoreType.DMA,
            pltpu.SemaphoreType.DMA,
            pltpu.SemaphoreType.DMA((15,)),
            pltpu.SemaphoreType.DMA,
            pltpu.SemaphoreType.DMA((tiles, 4)),
            pltpu.SemaphoreType.DMA((tiles, 11)),
            pltpu.SemaphoreType.DMA((half,)),
            pltpu.SemaphoreType.DMA((half,)),
        ],
        compiler_params=pltpu.CompilerParams(
            collective_id=0, has_side_effects=True, vmem_limit_bytes=48 * 2**20),
        name="correct",
    )(proj, dh, ids)


def solution(mesh):
    placed = (P("atom", None, "row"), P("atom", "row"), P("atom", None, None, None))
    return jax.shard_map(
        on_device, mesh=mesh, in_specs=placed, out_specs=P("row", ("col", "atom")), check_vma=False
    )
```

time: 273 us -> 54.1 us (0.20)
  the two profiles are of different devices: /device:TPU:1 before, /device:TPU:320 now
where the time goes in v1:
time: 54.1 us; the launch traced here: 53.9 us
  Pallas kernels  45.6 us (84%)
  local copies, waits for them, and re-layouts  8.27 us (15%)
    pallas_call x1, Pallas kernels, on_device(): pl.pallas_call(kernel, out_shape=jax.ShapeDtypeStruct((rows, half * BT),...  45.6 us
    unnamed x4, local copies, waits for them, and re-layouts  6.7 us

profile of v1, /device:TPU:320, one launch (start us, length us, event | category | flops | bytes accessed | tf_op | source)
XLA Modules:
  0.0 53.9 jit_solution(4954865841728857049)
XLA Ops:
  0.0 0.7 %broadcast_in_dim.3 = s32[12,6,6]{0,2,1:T(8,128)S(1)} broadcast(s32[12,6]{0,1:T(8,128)} %param.4), dimensions={0,1} | broadcast | bytes 2016 | tf_op jit(solution)/shard_map/broadcast_in_dim | solution.py:275
  0.7 0.1 copy.8
  0.8 0.7 %tile.4 = s32[12,6,6]{0,2,1:T(8,128)S(1)} broadcast(s32[12,6]{0,1:T(8,128)} %param.4), dimensions={0,2} | broadcast | bytes 2016 | tf_op jit(solution)/shard_map/tile | solution.py:274
  1.5 0.1 copy.7
  1.6 0.0 copy-start
  1.6 5.7 %copy.9.dh = f32[59,8,13,13]{3,2,1,0:T(8,128)} copy(f32[59,8,13,13]{0,1,3,2:T(8,128)} %param.5) | data formatting | bytes 638144 | tf_op args[2]
  7.3 0.0 copy-done
  7.3 45.6 %correct.1 = f32[768,384]{1,0:T(8,128)S(1)} custom-call(bf16[12,104,768]{2,1,0:T(8,128)(2,1)S(1)} %copy-done, f32[59,8,13,13]{3,2,1,0:T(8,128)} %copy.9.dh, s32[32,128]{1,0:T(8,128)S(1)} %select_add_fusion.ids), custom_call_target="tpu_custom_call" | custom-call | tf_op jit(solution)/shard_map/correct/pallas_call | solution.py:279
  52.9 1.0 %copy.11 = f32[768,384]{1,0:T(8,128)} copy(f32[768,384]{1,0:T(8,128)S(1)} %correct.1) | data formatting | bytes 2359296
  (3 shorter events, 0.0 us)
Async XLA Ops:
  1.6 5.7 %copy-start = (bf16[12,104,768]{2,1,0:T(8,128)(2,1)S(1)}, bf16[12,104,768]{2,1,0:T(8,128)(2,1)}, u32[]{:S(2)}) copy-start(bf16[12,104,768]{2,1,0:T(8,128)(2,1)} %proj.1) | copy-start | bytes 5750788

commit v2 on v1

v2 whole, which is shorter than its diff:
```python
import functools

import jax
import jax.numpy as jnp
from jax import lax
from jax.experimental import pallas as pl
from jax.experimental.pallas import tpu as pltpu
from jax.sharding import PartitionSpec as P

MESH = pl.DeviceIdType.MESH
BT = 128
PAD = 16


def kernel(proj, dht, nbh, out, nbt, pbuf, colb, dhv, tab, blocks, pt, sel, q, acc, xsend, xrecv,
           colx, col_s, fnd, fnd_s, lsem, dsem, isem, nsend, nrecv, rsem, ssem, xssem, xrsem):
    slots, ap, _ = proj.shape
    npj, _, atb, nats = dht.shape
    tiles = pbuf.shape[0]
    half = tiles // 2
    part = slots // 6
    row, c, a = lax.axis_index("row"), lax.axis_index("col"), lax.axis_index("atom")
    x, h, k = row // 4, (row // 2) % 2, row % 2
    xs, hs, ks = c // 4, (c // 2) % 2, c % 2
    is_root = row == c
    root_chip = (row // 2) == (c // 2)
    is_twin = root_chip & (row != c)
    e = (x - xs) % 4

    def dev(x_, h_, k_):
        return (x_ * 4 + h_ * 2 + k_, c, a)

    def tile_of(t):
        return (t + half * (1 - a)) % tiles

    bar = pltpu.get_barrier_semaphore()
    for i in range(1, 16):
        pl.semaphore_signal(bar, inc=1, device_id=((row + i) % 16, c, a), device_id_type=MESH)
    pl.semaphore_signal(bar, inc=1, device_id=(row, c, 1 - a), device_id_type=MESH)

    loads = [
        pltpu.make_async_copy(proj.at[:, :, pl.ds(i * BT, BT)], pbuf.at[i], lsem.at[i])
        for i in range(tiles)
    ]
    for cp in loads:
        cp.start()
    dcopy = pltpu.make_async_copy(dht, dhv, dsem)
    dcopy.start()
    ncopy = pltpu.make_async_copy(nbh, nbt, isem)
    ncopy.start()

    def piece(buf, i, p):
        return buf.at[i, pl.ds(part * p, part)]

    def send(src, t, p, slot, target):
        return pltpu.make_async_remote_copy(
            src_ref=src, dst_ref=piece(colb, t, p), send_sem=ssem.at[t, slot],
            recv_sem=rsem.at[t, p], device_id=target, device_id_type=MESH)

    def root_ids(i):
        return pltpu.make_async_remote_copy(
            src_ref=nbt, dst_ref=colx, send_sem=nsend.at[i - 1],
            recv_sem=nrecv, device_id=((row + i) % 16, c, a), device_id_type=MESH)

    def spread_out(src, i, t):
        return [send(piece(src, i, 2 * g + b), t, 2 * g + b, 2 * g + b,
                     dev((xs + 1 + g) % 4, hs, t % 2))
                for b in range(2) for g in (1, 0, 2)]

    def to_twin(t):
        return [send(piece(pbuf, tile_of(t), p), t, p, 6 + p, dev(xs, hs, 1 - ks))
                for p in range(6)]

    @pl.when(is_root)
    def _():
        for cp in loads:
            cp.wait()
        ncopy.wait()
        pl.semaphore_wait(bar, 16)
        for cp in spread_out(pbuf, tile_of(0), 0):
            cp.start()

        def odd(i, carry):
            for cp in to_twin(2 * i + 1):
                cp.start()
            return carry

        lax.fori_loop(0, half, odd, 0)
        for i in range(1, 16):
            root_ids(i).start()
        pltpu.make_async_copy(nbt, colx, nrecv).start()

        def even(i, carry):
            for cp in spread_out(pbuf, tile_of(2 * i), 2 * i):
                cp.start()
            return carry

        lax.fori_loop(1, half, even, 0)

        def rest(t, carry):
            @pl.when(t % 2 == 0)
            def _():
                for cp in to_twin(t):
                    cp.start()

            for p in range(6):
                pltpu.make_async_copy(
                    piece(pbuf, tile_of(t), p), piece(colb, t, p), rsem.at[t, p]).start()
            return carry

        lax.fori_loop(0, tiles, rest, 0)

    def arrived(t, p):
        pltpu.make_async_copy(piece(colb, t, p), piece(colb, t, p), rsem.at[t, p]).wait()

    def relay(t):
        return (k == t % 2) & jnp.logical_not(root_chip)

    def relay_first(t, b):
        p = 2 * jnp.maximum(e - 1, 0) + b
        mine = piece(colb, t, p)
        cross = send(mine, t, p, 6 + b, dev(x, 1 - h, k))
        along = [(send(mine, t, p, 8 + 3 * b + n, dev((x + d) % 4, h, k)),
                  ((e + d) % 4 != 0) | (h != hs))
                 for n, d in enumerate((2, 1, 3))]
        twin = send(mine, t, p, p, dev(x, h, 1 - k))
        return p, cross, along, twin

    def relay_rest(t):
        return [(p, (e == 0) | (e != p // 2 + 1),
                 send(piece(colb, t, p), t, p, p, dev(x, h, 1 - k))) for p in range(6)]

    def forward_first(t):
        @pl.when(relay(t) & (e > 0))
        def _():
            for b in range(2):
                p, cross, along, twin = relay_first(t, b)
                arrived(t, p)

                @pl.when(h == hs)
                def _():
                    cross.start()

                for cp, needed in along:
                    @pl.when(needed)
                    def _():
                        cp.start()

                twin.start()

    def forward_rest(t):
        @pl.when(relay(t))
        def _():
            for p, other, cp in relay_rest(t):
                @pl.when(other)
                def _():
                    arrived(t, p)
                    cp.start()

        @pl.when(jnp.logical_not(relay(t) | (is_twin & (t % 2 == 1))))
        def _():
            for p in range(6):
                arrived(t, p)

    ridx = lax.broadcasted_iota(jnp.int32, (npj * atb, BT), 0)
    cidx = lax.broadcasted_iota(jnp.int32, (npj * atb, BT), 1)
    order = (ridx & 7) * npj + (ridx >> 3) == cidx
    order = order.astype(jnp.float32).astype(jnp.bfloat16)
    turn = (((0,), (0,)), ((), ()))
    dcopy.wait()
    tab[:, npj:, :] = jnp.zeros((nats, PAD - npj, BT), jnp.float32)
    for i in range(npj):
        v = dhv[i].reshape(npj * atb, nats)
        hi = v.astype(jnp.bfloat16)
        lo = (v - hi.astype(jnp.float32)).astype(jnp.bfloat16)
        rows_i = lax.dot_general(hi, order, turn, preferred_element_type=jnp.float32)
        rows_i += lax.dot_general(lo, order, turn, preferred_element_type=jnp.float32)
        tab[:, i, :] = rows_i
    ridx = lax.broadcasted_iota(jnp.int32, (BT, BT), 0)
    cidx = lax.broadcasted_iota(jnp.int32, (BT, BT), 1)
    inside = cidx - (ridx >> 4) * npj
    inside = (inside >= 0) & (inside < npj)
    blocks[...] = inside.astype(jnp.float32).astype(jnp.bfloat16)

    @pl.when(jnp.logical_not(is_root))
    def _():
        for cp in loads:
            cp.wait()
        ncopy.wait()
        pl.semaphore_wait(bar, 16)

    @pl.when(is_twin)
    def _():
        def step(i, carry):
            t = 2 * i + 1
            for p in range(6):
                arrived(t, p)
            for cp in spread_out(colb, t, t):
                cp.start()
            return carry

        lax.fori_loop(0, half, step, 0)

    pidx = lax.broadcasted_iota(jnp.int32, (ap, BT), 0)
    sidx = lax.broadcasted_iota(jnp.int32, (ap, BT), 1)
    spread = ((sidx >> 4) * npj + (sidx & 15) == pidx) & ((sidx & 15) < npj)
    spread = spread.astype(jnp.float32).astype(jnp.bfloat16)

    def flip(u, carry):
        for l in range(slots):
            pt[u, l] = lax.dot_general(
                pbuf[u, l], spread, turn, preferred_element_type=jnp.float32).astype(jnp.bfloat16)
        pt[u, slots] = jnp.zeros((BT, BT), jnp.bfloat16)
        return carry

    lax.fori_loop(0, tiles, flip, 0)

    for t in range(4):
        forward_first(t)

    pltpu.make_async_copy(nbt, colx, nrecv).wait()
    ccopy = pltpu.make_async_copy(colx, col_s, isem)
    ccopy.start()
    ccopy.wait()
    rows_l = nbt[...]
    lidx = lax.broadcasted_iota(jnp.int32, (tiles, slots), 1)
    fidx = lax.broadcasted_iota(jnp.int32, (tiles, BT), 1)
    found = jnp.full((tiles, BT), slots, jnp.int32)
    for t in range(tiles):
        for m in range(slots):
            cs = col_s[t, m]
            hit = jnp.where((rows_l == cs) & (cs >= 0), lidx, slots)
            hit = jnp.min(hit, axis=1, keepdims=True)
            found = jnp.where(fidx == t * slots + m, hit, found)
    fnd[...] = found
    fcopy = pltpu.make_async_copy(fnd, fnd_s, isem)
    fcopy.start()
    fcopy.wait()

    def exchange(t):
        return pltpu.make_async_remote_copy(
            src_ref=xsend.at[t], dst_ref=xrecv.at[t], send_sem=xssem.at[t], recv_sem=xrsem.at[t],
            device_id=(row, c, 1 - a), device_id_type=MESH)

    def step(t, carry):
        forward_rest(t)

        @pl.when(t == 0)
        def _():
            forward_first(4)

        tile = tile_of(t)
        mask = blocks[...]
        for m in range(slots):
            v = tab[jnp.clip(col_s[tile, m] - a * nats, 0, nats - 1)]
            hi = v.astype(jnp.bfloat16)
            lo = (v - hi.astype(jnp.float32)).astype(jnp.bfloat16)
            hi = jnp.concatenate([hi] * atb, axis=0) * mask
            lo = jnp.concatenate([lo] * atb, axis=0) * mask
            piece = colb[t, m]
            prod = jnp.dot(hi[:, :ap], piece, preferred_element_type=jnp.float32)
            prod += jnp.dot(lo[:, :ap], piece, preferred_element_type=jnp.float32)
            q[m * BT:(m + 1) * BT, :] = prod.astype(jnp.bfloat16)
        for u in range(tiles):
            for m in range(slots):
                l = fnd_s[u, tile * slots + m]
                sel[u * BT:(u + 1) * BT, m * BT:(m + 1) * BT] = pt[u, l]
        block = jnp.dot(sel[...], q[...], preferred_element_type=jnp.float32)

        @pl.when(t < half)
        def _():
            xsend[t] = block.astype(jnp.bfloat16)
            exchange(t).start()

        @pl.when(t >= half)
        def _():
            acc[t - half] = block

        @pl.when(t == 0)
        def _():
            forward_first(5)

        return carry

    lax.fori_loop(0, tiles, step, 0)

    for j in range(half):
        exchange(j).wait_recv()
        out[:, j * BT:(j + 1) * BT] = acc[j] + xrecv[j].astype(jnp.float32)

    for j in range(half):
        exchange(j).wait_send()

    @pl.when(is_root)
    def _():
        for i in range(1, 16):
            root_ids(i).wait_send()

        def drain(t, carry):
            @pl.when(t % 2 == 0)
            def _():
                for cp in spread_out(pbuf, tile_of(t), t):
                    cp.wait_send()

            for cp in to_twin(t):
                cp.wait_send()
            return carry

        lax.fori_loop(0, tiles, drain, 0)

    @pl.when(is_twin)
    def _():
        def drain(i, carry):
            for cp in spread_out(colb, 2 * i + 1, 2 * i + 1):
                cp.wait_send()
            return carry

        lax.fori_loop(0, half, drain, 0)

    def drain(t, carry):
        @pl.when(relay(t))
        def _():
            @pl.when(e > 0)
            def _():
                for b in range(2):
                    p, cross, along, twin = relay_first(t, b)

                    @pl.when(h == hs)
                    def _():
                        cross.wait_send()

                    for cp, needed in along:
                        @pl.when(needed)
                        def _():
                            cp.wait_send()

                    twin.wait_send()

            for p, other, cp in relay_rest(t):
                @pl.when(other)
                def _():
                    cp.wait_send()

        return carry

    lax.fori_loop(0, tiles, drain, 0)


def on_device(proj, nbr, dh):
    slots, ap, rows = proj.shape
    tiles = nbr.shape[1]
    nats, atb, npj, _ = dh.shape
    half = tiles // 2
    dht = jnp.transpose(dh, (2, 3, 1, 0))
    bf, f32 = jnp.bfloat16, jnp.float32
    return pl.pallas_call(
        kernel,
        out_shape=jax.ShapeDtypeStruct((rows, half * BT), f32),
        in_specs=[pl.BlockSpec(memory_space=pltpu.HBM)] * 3,
        out_specs=pl.BlockSpec(memory_space=pltpu.VMEM),
        scratch_shapes=[
            pltpu.VMEM((tiles, slots), jnp.int32),
            pltpu.VMEM((tiles, slots, ap, BT), bf),
            pltpu.VMEM((tiles, slots, ap, BT), bf),
            pltpu.VMEM(dht.shape, f32),
            pltpu.VMEM((nats, PAD, BT), f32),
            pltpu.VMEM((BT, BT), bf),
            pltpu.VMEM((tiles, slots + 1, BT, BT), bf),
            pltpu.VMEM((rows, slots * BT), bf),
            pltpu.VMEM((slots * BT, BT), bf),
            pltpu.VMEM((half, rows, BT), f32),
            pltpu.VMEM((half, rows, BT), bf),
            pltpu.VMEM((half, rows, BT), bf),
            pltpu.VMEM((tiles, slots), jnp.int32),
            pltpu.SMEM((tiles, slots), jnp.int32),
            pltpu.VMEM((tiles, BT), jnp.int32),
            pltpu.SMEM((tiles, BT), jnp.int32),
            pltpu.SemaphoreType.DMA((tiles,)),
            pltpu.SemaphoreType.DMA,
            pltpu.SemaphoreType.DMA,
            pltpu.SemaphoreType.DMA((15,)),
            pltpu.SemaphoreType.DMA,
            pltpu.SemaphoreType.DMA((tiles, 6)),
            pltpu.SemaphoreType.DMA((tiles, 14)),
            pltpu.SemaphoreType.DMA((half,)),
            pltpu.SemaphoreType.DMA((half,)),
        ],
        compiler_params=pltpu.CompilerParams(
            collective_id=0, has_side_effects=True, vmem_limit_bytes=56 * 2**20),
        name="correct",
    )(proj, dht, nbr.T)


def solution(mesh):
    placed = (P("atom", None, "row"), P("atom", "row"), P("atom", None, None, None))
    return jax.shard_map(
        on_device, mesh=mesh, in_specs=placed, out_specs=P("row", ("col", "atom")), check_vma=False
    )
```

time: 54.1 us -> 46.1 us (0.85)
  the two profiles are of different devices: /device:TPU:320 before, /device:TPU:224 now
where the time goes in v2:
time: 46.1 us; the launch traced here: 45.9 us
  Pallas kernels  43.6 us (95%)
  local copies, waits for them, and re-layouts  2.36 us (5%)
    pallas_call x1, Pallas kernels, on_device(): pl.pallas_call(kernel, out_shape=jax.ShapeDtypeStruct((rows, half * BT),...  43.6 us
    unnamed x1, local copies, waits for them, and re-layouts  2.36 us

profile of v2, /device:TPU:224, one launch (start us, length us, event | category | flops | bytes accessed | tf_op | source)
XLA Modules:
  0.0 45.9 jit_solution(14964653348012712898)
XLA Ops:
  0.0 43.6 %correct.1 = f32[768,384]{1,0:T(8,128)} custom-call(bf16[12,104,768]{2,1,0:T(8,128)(2,1)} %proj.1, f32[13,13,8,59]{3,2,1,0:T(8,128)} %bitcast.2, s32[6,12]{1,0:T(8,128)} %bitcast.3), custom_call_target="tpu_custom_call" | custom-call | tf_op jit(solution)/shard_map/correct/pallas_call | solution.py:356
  43.6 2.4 %copy.5 = f32[768,384]{1,0:T(8,128)} copy(f32[768,384]{1,0:T(8,128)} %correct.1) | data formatting | bytes 2359296

commit v3 on v2

v3 whole, which is shorter than its diff:
```python
import functools

import jax
import jax.numpy as jnp
from jax import lax
from jax.experimental import pallas as pl
from jax.experimental.pallas import tpu as pltpu
from jax.sharding import PartitionSpec as P

MESH = pl.DeviceIdType.MESH
BT = 128
PAD = 16


def kernel(proj, dht, nbh, own, theirs, nbt, pbuf, colb, dhv, tab, blocks, pt, q, acc, xsend,
           colx, col_s, fnd, fnd_s, lsem, dsem, isem, nsend, nrecv, rsem, ssem, xssem, xrsem, osem):
    slots, ap, _ = proj.shape
    npj, _, atb, nats = dht.shape
    tiles = pbuf.shape[0]
    half = tiles // 2
    share = slots // 6
    row, c, a = lax.axis_index("row"), lax.axis_index("col"), lax.axis_index("atom")
    x, h, k = row // 4, (row // 2) % 2, row % 2
    xs, hs, ks = c // 4, (c // 2) % 2, c % 2
    is_root = row == c
    root_chip = (row // 2) == (c // 2)
    is_twin = root_chip & (row != c)
    e = (x - xs) % 4

    def dev(x_, h_, k_):
        return (x_ * 4 + h_ * 2 + k_, c, a)

    def tile_of(t):
        return (t + half * (1 - a)) % tiles

    bar = pltpu.get_barrier_semaphore()
    for i in range(1, 16):
        pl.semaphore_signal(bar, inc=1, device_id=((row + i) % 16, c, a), device_id_type=MESH)
    pl.semaphore_signal(bar, inc=1, device_id=(row, c, 1 - a), device_id_type=MESH)

    loads = [
        pltpu.make_async_copy(proj.at[:, :, pl.ds(i * BT, BT)], pbuf.at[i], lsem.at[i])
        for i in range(tiles)
    ]
    for cp in loads:
        cp.start()
    dcopy = pltpu.make_async_copy(dht, dhv, dsem)
    dcopy.start()
    ncopy = pltpu.make_async_copy(nbh, nbt, isem)
    ncopy.start()

    def piece(buf, i, p):
        return buf.at[i, pl.ds(share * p, share)]

    def send(src, t, p, slot, target):
        return pltpu.make_async_remote_copy(
            src_ref=src, dst_ref=piece(colb, t, p), send_sem=ssem.at[t, slot],
            recv_sem=rsem.at[t, p], device_id=target, device_id_type=MESH)

    def root_ids(i):
        return pltpu.make_async_remote_copy(
            src_ref=nbt, dst_ref=colx, send_sem=nsend.at[i - 1],
            recv_sem=nrecv, device_id=((row + i) % 16, c, a), device_id_type=MESH)

    def spread_out(src, i, t, b):
        return [send(piece(src, i, 2 * g + b), t, 2 * g + b, 2 * g + b,
                     dev((xs + 1 + g) % 4, hs, b)) for g in ((1, 0, 2), (2, 1, 0))[b]]

    def to_twin(t, b):
        return [send(piece(pbuf, tile_of(t), 2 * g + b), t, 2 * g + b, 6 + 2 * g + b,
                     dev(xs, hs, 1 - ks)) for g in (1, 0, 2)]

    @pl.when(is_root)
    def _():
        for cp in loads:
            cp.wait()
        ncopy.wait()
        pl.semaphore_wait(bar, 16)

        def first(t, carry):
            for cp in to_twin(t, 1):
                cp.start()
            for cp in spread_out(pbuf, tile_of(t), t, 0):
                cp.start()
            return carry

        lax.fori_loop(0, 2, first, 0)
        for i in range(1, 16):
            root_ids(i).start()
        pltpu.make_async_copy(nbt, colx, nrecv).start()
        lax.fori_loop(2, tiles, first, 0)

        def rest(t, carry):
            for cp in to_twin(t, 0):
                cp.start()
            for p in range(6):
                pltpu.make_async_copy(
                    piece(pbuf, tile_of(t), p), piece(colb, t, p), rsem.at[t, p]).start()
            return carry

        lax.fori_loop(0, tiles, rest, 0)

    def arrived(t, p):
        pltpu.make_async_copy(piece(colb, t, p), piece(colb, t, p), rsem.at[t, p]).wait()

    relay = jnp.logical_not(root_chip)

    def relay_first(t):
        p = 2 * jnp.maximum(e - 1, 0) + k
        mine = piece(colb, t, p)
        cross = send(mine, t, p, 6, dev(x, 1 - h, k))
        hops = [n + 1 + k * (2 - 2 * n) for n in range(3)]
        along = [(send(mine, t, p, 7 + n, dev((x + d) % 4, h, k)),
                  ((e + d) % 4 != 0) | (h != hs)) for n, d in enumerate(hops)]
        twin = send(mine, t, p, p, dev(x, h, 1 - k))
        return p, cross, along, twin

    def relay_rest(t):
        return [(2 * g + k, e != g + 1,
                 send(piece(colb, t, 2 * g + k), t, 2 * g + k, 2 * g + k, dev(x, h, 1 - k)))
                for g in range(3)]

    def forward_first(t):
        @pl.when(relay & (e > 0))
        def _():
            p, cross, along, twin = relay_first(t)
            arrived(t, p)

            @pl.when(h == hs)
            def _():
                cross.start()

            for cp, needed in along:
                @pl.when(needed)
                def _():
                    cp.start()

            twin.start()

    def forward_rest(t):
        @pl.when(relay)
        def _():
            for p, other, cp in relay_rest(t):
                @pl.when(other)
                def _():
                    arrived(t, p)
                    cp.start()

    def complete(t):
        @pl.when(relay)
        def _():
            for g in range(3):
                arrived(t, 2 * g + 1 - k)

        @pl.when(root_chip)
        def _():
            for g in range(3):
                arrived(t, 2 * g)

        @pl.when(is_root)
        def _():
            for g in range(3):
                arrived(t, 2 * g + 1)

    ridx = lax.broadcasted_iota(jnp.int32, (npj * atb, BT), 0)
    cidx = lax.broadcasted_iota(jnp.int32, (npj * atb, BT), 1)
    order = (ridx & 7) * npj + (ridx >> 3) == cidx
    order = order.astype(jnp.float32).astype(jnp.bfloat16)
    turn = (((0,), (0,)), ((), ()))
    dcopy.wait()
    tab[:, npj:, :] = jnp.zeros((nats, PAD - npj, BT), jnp.float32)
    for i in range(npj):
        v = dhv[i].reshape(npj * atb, nats)
        hi = v.astype(jnp.bfloat16)
        lo = (v - hi.astype(jnp.float32)).astype(jnp.bfloat16)
        rows_i = lax.dot_general(hi, order, turn, preferred_element_type=jnp.float32)
        rows_i += lax.dot_general(lo, order, turn, preferred_element_type=jnp.float32)
        tab[:, i, :] = rows_i
    ridx = lax.broadcasted_iota(jnp.int32, (BT, BT), 0)
    cidx = lax.broadcasted_iota(jnp.int32, (BT, BT), 1)
    inside = cidx - (ridx >> 4) * npj
    inside = (inside >= 0) & (inside < npj)
    blocks[...] = inside.astype(jnp.float32).astype(jnp.bfloat16)

    @pl.when(jnp.logical_not(is_root))
    def _():
        for cp in loads:
            cp.wait()
        ncopy.wait()
        pl.semaphore_wait(bar, 16)

    @pl.when(is_twin)
    def _():
        def first(t, carry):
            for g in (1, 0, 2):
                arrived(t, 2 * g + 1)
            for cp in spread_out(colb, t, t, 1):
                cp.start()
            return carry

        lax.fori_loop(0, tiles, first, 0)

    pidx = lax.broadcasted_iota(jnp.int32, (ap, BT), 0)
    sidx = lax.broadcasted_iota(jnp.int32, (ap, BT), 1)
    spread = ((sidx >> 4) * npj + (sidx & 15) == pidx) & ((sidx & 15) < npj)
    spread = spread.astype(jnp.float32).astype(jnp.bfloat16)

    def flip(u, carry):
        for l in range(slots):
            pt[u, l] = lax.dot_general(
                pbuf[u, l], spread, turn, preferred_element_type=jnp.float32).astype(jnp.bfloat16)
        pt[u, slots] = jnp.zeros((BT, BT), jnp.bfloat16)
        return carry

    lax.fori_loop(0, tiles, flip, 0)

    for t in range(4):
        forward_first(t)

    pltpu.make_async_copy(nbt, colx, nrecv).wait()
    ccopy = pltpu.make_async_copy(colx, col_s, isem)
    ccopy.start()
    ccopy.wait()
    rows_l = nbt[...]
    lidx = lax.broadcasted_iota(jnp.int32, (tiles, slots), 1)
    fidx = lax.broadcasted_iota(jnp.int32, (tiles, BT), 1)
    found = jnp.full((tiles, BT), slots, jnp.int32)
    for t in range(tiles):
        for m in range(slots):
            cs = col_s[t, m]
            hit = jnp.where((rows_l == cs) & (cs >= 0), lidx, slots)
            hit = jnp.min(hit, axis=1, keepdims=True)
            found = jnp.where(fidx == t * slots + m, hit, found)
    fnd[...] = found
    fcopy = pltpu.make_async_copy(fnd, fnd_s, isem)
    fcopy.start()
    fcopy.wait()

    def part(ref, j, u):
        return ref.at[pl.ds(u * BT, BT), pl.ds(pl.multiple_of(j * BT, BT), BT)]

    def exchange(j, u):
        return pltpu.make_async_remote_copy(
            src_ref=xsend.at[j, u], dst_ref=part(theirs, j, u), send_sem=xssem.at[j, u],
            recv_sem=xrsem.at[j, u], device_id=(row, c, 1 - a), device_id_type=MESH)

    def keep(j, u):
        return pltpu.make_async_copy(acc.at[j, u], part(own, j, u), osem.at[j, u])

    forward_rest(0)
    forward_first(4)

    def step(t, carry):
        complete(t)

        @pl.when(t + 1 < tiles)
        def _():
            forward_rest(t + 1)

        @pl.when(t == 0)
        def _():
            forward_first(5)

        tile = tile_of(t)
        mask = blocks[...]
        for m in range(slots):
            v = tab[jnp.clip(col_s[tile, m] - a * nats, 0, nats - 1)]
            hi = v.astype(jnp.bfloat16)
            lo = (v - hi.astype(jnp.float32)).astype(jnp.bfloat16)
            hi = jnp.concatenate([hi] * atb, axis=0) * mask
            lo = jnp.concatenate([lo] * atb, axis=0) * mask
            piece = colb[t, m]
            prod = jnp.dot(hi[:, :ap], piece, preferred_element_type=jnp.float32)
            prod += jnp.dot(lo[:, :ap], piece, preferred_element_type=jnp.float32)
            q[m * BT:(m + 1) * BT, :] = prod.astype(jnp.bfloat16)
        for u in range(tiles):
            lhs = [pt[u, fnd_s[u, tile * slots + m]] for m in range(slots)]
            block = jnp.dot(jnp.concatenate(lhs, axis=1), q[...],
                            preferred_element_type=jnp.float32)

            @pl.when(t < half)
            def _():
                xsend[t, u] = block.astype(jnp.bfloat16)
                exchange(t, u).start()

            @pl.when(t >= half)
            def _():
                acc[t - half, u] = block
                keep(t - half, u).start()

        return carry

    lax.fori_loop(0, tiles, step, 0)

    def finish(j, carry):
        for u in range(tiles):
            keep(j, u).wait()
            exchange(j, u).wait_send()
            exchange(j, u).wait_recv()
        return carry

    lax.fori_loop(0, half, finish, 0)

    @pl.when(is_root)
    def _():
        for i in range(1, 16):
            root_ids(i).wait_send()

        def drain(t, carry):
            for b in range(2):
                for cp in to_twin(t, b):
                    cp.wait_send()
            for cp in spread_out(pbuf, tile_of(t), t, 0):
                cp.wait_send()
            return carry

        lax.fori_loop(0, tiles, drain, 0)

    @pl.when(is_twin)
    def _():
        def drain(t, carry):
            for cp in spread_out(colb, t, t, 1):
                cp.wait_send()
            return carry

        lax.fori_loop(0, tiles, drain, 0)

    @pl.when(relay)
    def _():
        def drain(t, carry):
            @pl.when(e > 0)
            def _():
                p, cross, along, twin = relay_first(t)

                @pl.when(h == hs)
                def _():
                    cross.wait_send()

                for cp, needed in along:
                    @pl.when(needed)
                    def _():
                        cp.wait_send()

                twin.wait_send()

            for p, other, cp in relay_rest(t):
                @pl.when(other)
                def _():
                    cp.wait_send()

            return carry

        lax.fori_loop(0, tiles, drain, 0)


def on_device(proj, nbr, dh):
    slots, ap, rows = proj.shape
    tiles = nbr.shape[1]
    nats, atb, npj, _ = dh.shape
    half = tiles // 2
    dht = jnp.transpose(dh, (2, 3, 1, 0))
    bf, f32 = jnp.bfloat16, jnp.float32
    own, theirs = pl.pallas_call(
        kernel,
        out_shape=[jax.ShapeDtypeStruct((rows, half * BT), f32),
                   jax.ShapeDtypeStruct((rows, half * BT), bf)],
        in_specs=[pl.BlockSpec(memory_space=pltpu.HBM)] * 3,
        out_specs=[pl.BlockSpec(memory_space=pl.ANY)] * 2,
        scratch_shapes=[
            pltpu.VMEM((tiles, slots), jnp.int32),
            pltpu.VMEM((tiles, slots, ap, BT), bf),
            pltpu.VMEM((tiles, slots, ap, BT), bf),
            pltpu.VMEM(dht.shape, f32),
            pltpu.VMEM((nats, PAD, BT), f32),
            pltpu.VMEM((BT, BT), bf),
            pltpu.VMEM((tiles, slots + 1, BT, BT), bf),
            pltpu.VMEM((slots * BT, BT), bf),
            pltpu.VMEM((half, tiles, BT, BT), f32),
            pltpu.VMEM((half, tiles, BT, BT), bf),
            pltpu.VMEM((tiles, slots), jnp.int32),
            pltpu.SMEM((tiles, slots), jnp.int32),
            pltpu.VMEM((tiles, BT), jnp.int32),
            pltpu.SMEM((tiles, BT), jnp.int32),
            pltpu.SemaphoreType.DMA((tiles,)),
            pltpu.SemaphoreType.DMA,
            pltpu.SemaphoreType.DMA,
            pltpu.SemaphoreType.DMA((15,)),
            pltpu.SemaphoreType.DMA,
            pltpu.SemaphoreType.DMA((tiles, 6)),
            pltpu.SemaphoreType.DMA((tiles, 12)),
            pltpu.SemaphoreType.DMA((half, tiles)),
            pltpu.SemaphoreType.DMA((half, tiles)),
            pltpu.SemaphoreType.DMA((half, tiles)),
        ],
        compiler_params=pltpu.CompilerParams(
            collective_id=0, has_side_effects=True, vmem_limit_bytes=56 * 2**20),
        name="correct",
    )(proj, dht, nbr.T)
    return own + theirs.astype(f32)


def solution(mesh):
    placed = (P("atom", None, "row"), P("atom", "row"), P("atom", None, None, None))
    return jax.shard_map(
        on_device, mesh=mesh, in_specs=placed, out_specs=P("row", ("col", "atom")), check_vma=False
    )
```

time: 46.1 us -> 46 us (level)
  the two profiles are of different devices: /device:TPU:224 before, /device:TPU:18 now
where the time goes in v3:
time: 46 us; the launch traced here: 45.8 us
  Pallas kernels  43.3 us (94%)
  other arithmetic  2.53 us (5%)
    pallas_call x1, Pallas kernels, on_device(): pl.pallas_call(kernel, out_shape=[jax.ShapeDtypeStruct((rows, half * BT),...  43.3 us
    add x1, other arithmetic, on_device(): return own + theirs.astype(f32)  2.53 us

profile of v3, /device:TPU:18, one launch (start us, length us, event | category | flops | bytes accessed | tf_op | source)
XLA Modules:
  0.0 45.8 jit_solution(5747579585744995220)
XLA Ops:
  0.0 43.3 %correct.1 = (f32[768,384]{1,0:T(8,128)}, bf16[768,384]{1,0:T(8,128)(2,1)}) custom-call(bf16[12,104,768]{2,1,0:T(8,128)(2,1)} %proj.1, f32[13,13,8,59]{3,2,1,0:T(8,128)} %bitcast.2, s32[6,12]{1,0:T(8,128)} %bitcast.3), custom_call_target="tpu_custom_call" | custom-call | tf_op jit(solution)/shard_map/correct/pallas_call | solution.py:363
  43.3 2.5 %convert_add_fusion = f32[768,384]{1,0:T(8,128)} fusion(f32[768,384]{1,0:T(8,128)} %get-tuple-element.7, bf16[768,384]{1,0:T(8,128)(2,1)} %get-tuple-element.8), kind=kLoop, calls=%fused_computation | loop fusion | flops 589824 | bytes 2949120 | tf_op jit(solution)/shard_map/add | solution.py:399

commit v4 on v3

--- a/solution.py
+++ b/solution.py
@@ -77,9 +77,15 @@
         ncopy.wait()
         pl.semaphore_wait(bar, 16)
 
+        for cp in to_twin(0, 1):
+            cp.start()
+
         def first(t, carry):
-            for cp in to_twin(t, 1):
-                cp.start()
+            @pl.when(t + 1 < tiles)
+            def _():
+                for cp in to_twin(t + 1, 1):
+                    cp.start()
+
             for cp in spread_out(pbuf, tile_of(t), t, 0):
                 cp.start()
             return carry
@@ -214,7 +220,7 @@
 
     lax.fori_loop(0, tiles, flip, 0)
 
-    for t in range(4):
+    for t in range(3):
         forward_first(t)
 
     pltpu.make_async_copy(nbt, colx, nrecv).wait()
@@ -236,31 +242,21 @@
     fcopy.start()
     fcopy.wait()
 
-    def part(ref, j, u):
-        return ref.at[pl.ds(u * BT, BT), pl.ds(pl.multiple_of(j * BT, BT), BT)]
-
-    def exchange(j, u):
+    def part(ref, j, i):
+        return ref.at[pl.ds(2 * i, 2), :, pl.ds(pl.multiple_of(j * BT, BT), BT)]
+
+    def exchange(j, i):
         return pltpu.make_async_remote_copy(
-            src_ref=xsend.at[j, u], dst_ref=part(theirs, j, u), send_sem=xssem.at[j, u],
-            recv_sem=xrsem.at[j, u], device_id=(row, c, 1 - a), device_id_type=MESH)
-
-    def keep(j, u):
-        return pltpu.make_async_copy(acc.at[j, u], part(own, j, u), osem.at[j, u])
+            src_ref=xsend.at[j, pl.ds(2 * i, 2)], dst_ref=part(theirs, j, i), send_sem=xssem.at[j, i],
+            recv_sem=xrsem.at[j, i], device_id=(row, c, 1 - a), device_id_type=MESH)
+
+    def keep(j, i):
+        return pltpu.make_async_copy(acc.at[j, pl.ds(2 * i, 2)], part(own, j, i), osem.at[j, i])
 
     forward_rest(0)
-    forward_first(4)
 
     def step(t, carry):
         complete(t)
-
-        @pl.when(t + 1 < tiles)
-        def _():
-            forward_rest(t + 1)
-
-        @pl.when(t == 0)
-        def _():
-            forward_first(5)
-
         tile = tile_of(t)
         mask = blocks[...]
         for m in range(slots):
@@ -273,30 +269,54 @@
             prod = jnp.dot(hi[:, :ap], piece, preferred_element_type=jnp.float32)
             prod += jnp.dot(lo[:, :ap], piece, preferred_element_type=jnp.float32)
             q[m * BT:(m + 1) * BT, :] = prod.astype(jnp.bfloat16)
-        for u in range(tiles):
-            lhs = [pt[u, fnd_s[u, tile * slots + m]] for m in range(slots)]
-            block = jnp.dot(jnp.concatenate(lhs, axis=1), q[...],
-                            preferred_element_type=jnp.float32)
+        def two(i, carry):
+            blocks = []
+            for n in range(2):
+                u = 2 * i + n
+                lhs = [pt[u, fnd_s[u, tile * slots + m]] for m in range(slots)]
+                blocks.append(jnp.dot(jnp.concatenate(lhs, axis=1), q[...],
+                                      preferred_element_type=jnp.float32))
 
             @pl.when(t < half)
             def _():
-                xsend[t, u] = block.astype(jnp.bfloat16)
-                exchange(t, u).start()
+                for n in range(2):
+                    xsend[t, 2 * i + n] = blocks[n].astype(jnp.bfloat16)
 
             @pl.when(t >= half)
             def _():
-                acc[t - half, u] = block
-                keep(t - half, u).start()
+                for n in range(2):
+                    acc[t - half, 2 * i + n] = blocks[n]
+                keep(t - half, i).start()
+
+            return carry
+
+        lax.fori_loop(0, half, two, 0)
+
+        @pl.when(t == 0)
+        def _():
+            forward_first(3)
+            forward_first(4)
+            forward_rest(1)
+            forward_first(5)
+
+        @pl.when((t > 0) & (t + 1 < tiles))
+        def _():
+            forward_rest(t + 1)
+
+        @pl.when(t < half)
+        def _():
+            for i in range(half):
+                exchange(t, i).start()
 
         return carry
 
     lax.fori_loop(0, tiles, step, 0)
 
     def finish(j, carry):
-        for u in range(tiles):
-            keep(j, u).wait()
-            exchange(j, u).wait_send()
-            exchange(j, u).wait_recv()
+        for i in range(half):
+            keep(j, i).wait()
+            exchange(j, i).wait_send()
+            exchange(j, i).wait_recv()
         return carry
 
     lax.fori_loop(0, half, finish, 0)
@@ -362,8 +382,8 @@
     bf, f32 = jnp.bfloat16, jnp.float32
     own, theirs = pl.pallas_call(
         kernel,
-        out_shape=[jax.ShapeDtypeStruct((rows, half * BT), f32),
-                   jax.ShapeDtypeStruct((rows, half * BT), bf)],
+        out_shape=[jax.ShapeDtypeStruct((tiles, BT, half * BT), f32),
+                   jax.ShapeDtypeStruct((tiles, BT, half * BT), bf)],
         in_specs=[pl.BlockSpec(memory_space=pltpu.HBM)] * 3,
         out_specs=[pl.BlockSpec(memory_space=pl.ANY)] * 2,
         scratch_shapes=[
@@ -396,7 +416,7 @@
             collective_id=0, has_side_effects=True, vmem_limit_bytes=56 * 2**20),
         name="correct",
     )(proj, dht, nbr.T)
-    return own + theirs.astype(f32)
+    return (own + theirs.astype(f32)).reshape(rows, half * BT)
 
 
 def solution(mesh):

time: 46 us -> 45.5 us (0.989)
  Pallas kernels: 43.3 us -> 42.7 us
    pallas_call x1, Pallas kernels: 43.3 us -> 42.7 us  [on_device(): pl.pallas_call(kernel, out_shape=[jax.ShapeDtypeStruct((tiles, BT, half *...]
where the time goes in v4:
time: 45.5 us; the launch traced here: 45.3 us
  Pallas kernels  42.7 us (94%)
  other arithmetic  2.53 us (6%)
    pallas_call x1, Pallas kernels, on_device(): pl.pallas_call(kernel, out_shape=[jax.ShapeDtypeStruct((tiles, BT, half *...  42.7 us
    add x1, other arithmetic, on_device(): return (own + theirs.astype(f32)).reshape(rows, half * BT)  2.53 us

profile of v4, /device:TPU:18, one launch (start us, length us, event | category | flops | bytes accessed | tf_op | source)
XLA Modules:
  0.0 45.3 jit_solution(3654441328003206425)
XLA Ops:
  0.0 42.7 %correct.1 = (f32[6,128,384]{2,1,0:T(8,128)}, bf16[6,128,384]{2,1,0:T(8,128)(2,1)}) custom-call(bf16[12,104,768]{2,1,0:T(8,128)(2,1)} %proj.1, f32[13,13,8,59]{3,2,1,0:T(8,128)} %bitcast.3, s32[6,12]{1,0:T(8,128)} %bitcast.4), custom_call_target="tpu_custom_call" | custom-call | tf_op jit(solution)/shard_map/correct/pallas_call | solution.py:383
  42.7 2.5 %convert_add_fusion = f32[6,128,384]{2,1,0:T(8,128)} fusion(f32[6,128,384]{2,1,0:T(8,128)} %get-tuple-element.7, bf16[6,128,384]{2,1,0:T(8,128)(2,1)} %get-tuple-element.8), kind=kLoop, calls=%fused_computation | loop fusion | flops 589824 | bytes 2949120 | tf_op jit(solution)/shard_map/add | solution.py:419

commit v5 on v4

--- a/solution.py
+++ b/solution.py
@@ -90,11 +90,11 @@
                 cp.start()
             return carry
 
-        lax.fori_loop(0, 2, first, 0)
+        lax.fori_loop(0, 4, first, 0)
         for i in range(1, 16):
             root_ids(i).start()
         pltpu.make_async_copy(nbt, colx, nrecv).start()
-        lax.fori_loop(2, tiles, first, 0)
+        lax.fori_loop(4, tiles, first, 0)
 
         def rest(t, carry):
             for cp in to_twin(t, 0):

time: 45.5 us -> 46.7 us (1.026)
  the two profiles are of different devices: /device:TPU:18 before, /device:TPU:320 now
where the time goes in v5:
time: 46.7 us; the launch traced here: 46.5 us
  Pallas kernels  44 us (94%)
  other arithmetic  2.53 us (5%)
    pallas_call x1, Pallas kernels, on_device(): pl.pallas_call(kernel, out_shape=[jax.ShapeDtypeStruct((tiles, BT, half *...  44 us
    add x1, other arithmetic, on_device(): return (own + theirs.astype(f32)).reshape(rows, half * BT)  2.53 us

profile of v5, /device:TPU:320, one launch (start us, length us, event | category | flops | bytes accessed | tf_op | source)
XLA Modules:
  0.0 46.5 jit_solution(13782936111870894865)
XLA Ops:
  0.0 44.0 %correct.1 = (f32[6,128,384]{2,1,0:T(8,128)}, bf16[6,128,384]{2,1,0:T(8,128)(2,1)}) custom-call(bf16[12,104,768]{2,1,0:T(8,128)(2,1)} %proj.1, f32[13,13,8,59]{3,2,1,0:T(8,128)} %bitcast.3, s32[6,12]{1,0:T(8,128)} %bitcast.4), custom_call_target="tpu_custom_call" | custom-call | tf_op jit(solution)/shard_map/correct/pallas_call | solution.py:383
  44.0 2.5 %convert_add_fusion = f32[6,128,384]{2,1,0:T(8,128)} fusion(f32[6,128,384]{2,1,0:T(8,128)} %get-tuple-element.7, bf16[6,128,384]{2,1,0:T(8,128)(2,1)} %get-tuple-element.8), kind=kLoop, calls=%fused_computation | loop fusion | flops 589824 | bytes 2949120 | tf_op jit(solution)/shard_map/add | solution.py:419
